TPU v7x, 32 devices: a whole 2x2x4 slice. The times are simulated.
32 devices in a mesh: dp: 4 (over y, x), tm: 8 (over z, core).
Axes of the slice: x: 2, y: 2, z: 4, core: 2. Of those that a mesh axis runs over, the one named last changes fastest.
Arguments:
- pixels: bfloat16 [4, 8, 32, 192], P('dp', 'tm'), may hold values from -1 to 1
- counts: int32 [8, 4, 4], P('tm'), may hold values from 7 to 9, as said below
- clip_lengths: int32 [4, 4], P('dp'), may hold values from 1 to 17, 32 in all within a row
- in_weight: bfloat16 [3, 3, 3, 3, 128], replicated, may hold values from -0.625 to 0.625
- in_bias: float32 [128], replicated, may hold values from -3 to 3
- norm1_gain: float32 [128], replicated, may hold values from 0.5 to 1.5
- norm1_bias: float32 [128], replicated, may hold values from -3 to 3
- conv1_weight: bfloat16 [3, 3, 3, 128, 128], replicated, may hold values from -0.109375 to 0.109375
- norm2_gain: float32 [128], replicated, may hold values from 0.5 to 1.5
- norm2_bias: float32 [128], replicated, may hold values from -3 to 3
- conv2_weight: bfloat16 [3, 3, 3, 128, 128], replicated, may hold values from -0.109375 to 0.109375
- down_weight: bfloat16 [3, 3, 128, 128], replicated, may hold values from -0.1875 to 0.1875
Outputs:
- latents: bfloat16 [4, 8, 32, 2048], P('dp', 'tm')
Inputs may be any that keep to these rules, and one draw needn't show every extreme that they name: For each time block, every row and every column of counts sums to 32, and every row holds exactly one entry equal to 9. `clip_lengths`: each row sums to 32, and its longest clip has exactly 17 frames.
All inputs are finite; a program needn't handle non-finite values.
Results may differ from a plain program's by a relative error of at most 0.011.
Values may be sent and summed in bfloat16 or wider, within the bound.
A program may use at most 128 MiB of HBM per device.

v0:
```python
import functools

import jax
import jax.numpy as jnp
import numpy as np
from jax import lax
from jax.experimental import pallas as pl
from jax.experimental.pallas import tpu as pltpu
from jax.sharding import PartitionSpec as P

GROUPS = 32
HS = 32
PW = 16
RB = 4
CH = 128
LAGS = 3
EPS = 1e-06
MESH = pl.DeviceIdType.MESH
BF = jnp.bfloat16
F32 = jnp.float32
WIDE = 256
ROW = PW * 3
PIX = HS * PW


def tap_columns():
    table = np.full((LAGS * WIDE, CH), -100, np.int32)
    for kt in range(LAGS):
        for dy in range(3):
            for col in range(PW):
                for color in range(3):
                    r = kt * WIDE + dy * ROW + col * 3 + color
                    for dx in range(3):
                        table[r, ((kt * 3 + dy) * 3 + dx) * 3 + color] = col + 1 - dx
    return table


def group_sum(x):
    lane = lax.broadcasted_iota(jnp.int32, x.shape, 1)
    for step in (1, 2):
        ahead = pltpu.roll(x, CH - step, axis=1)
        behind = pltpu.roll(x, step, axis=1)
        x = x + jnp.where((lane & step) == 0, ahead, behind)
    return x


def kernel(
    n_dp,
    n_tm,
    counts,
    lengths,
    pixels,
    columns,
    in_w,
    vecs,
    w1_hbm,
    w2_hbm,
    wd_hbm,
    out,
    w1,
    w2,
    wd,
    toeplitz,
    placed,
    pix_in,
    pix_rows,
    xrows,
    lhs,
    base,
    mid,
    act,
    resid,
    mid_send,
    mid_halo,
    stats1,
    stats2,
    latent,
    packed,
    returned,
    gathered,
    w_sem,
    px_send,
    px_recv,
    st_send,
    st_recv,
    halo_send,
    halo_recv,
    back_send,
    back_recv,
):
    units = pixels.shape[0]
    per_frame = HS // RB
    span = units // per_frame
    cap = units // n_dp + 1
    me = lax.axis_index("dp")
    t = lax.axis_index("tm")
    clips = lengths.shape[0]

    barrier = pltpu.get_barrier_semaphore()

    def greet(d, column):
        pl.semaphore_signal(barrier, inc=1, device_id=(d, column), device_id_type=MESH)

    for k in range(1, n_tm):
        greet(me, lax.rem(t + k, n_tm))
    for k in range(1, n_dp):
        d = lax.rem(me + k, n_dp)
        greet(d, t)

        @pl.when(t > 0)
        def _():
            greet(d, t - 1)

        @pl.when(t < n_tm - 1)
        def _():
            greet(d, t + 1)

    weight_copies = [
        pltpu.make_async_copy(src, dst, w_sem.at[i])
        for i, (src, dst) in enumerate(((w1_hbm, w1), (w2_hbm, w2), (wd_hbm, wd)))
    ]
    for copy in weight_copies:
        copy.start()

    def recv_start_of(d, e):
        total = jnp.int32(0)
        for other in range(n_dp):
            total = total + jnp.where(other < d, counts[other, e], 0)
        return total

    send_start, send_end = [], []
    running = jnp.int32(0)
    for e in range(n_dp):
        send_start.append(running)
        running = running + counts[me, e]
        send_end.append(running)

    place_r = lax.broadcasted_iota(jnp.int32, (units, units), 0)
    place_i = lax.broadcasted_iota(jnp.int32, (units, units), 1)
    mine = pixels[...]
    for e in range(n_dp):
        turn = recv_start_of(me, e) - send_start[e]
        hit = (place_r == place_i + turn) & (place_i >= send_start[e]) & (place_i < send_end[e])
        placed[e] = jnp.dot(
            hit.astype(F32).astype(BF), mine, preferred_element_type=F32
        ).astype(BF)

    at_edge = (t == 0) | (t == n_tm - 1)

    @pl.when(at_edge)
    def _():
        pl.semaphore_wait(barrier, n_tm - 1 + 2 * (n_dp - 1))

    @pl.when(jnp.logical_not(at_edge))
    def _():
        pl.semaphore_wait(barrier, n_tm - 1 + 3 * (n_dp - 1))

    def pixel_copy(e, ahead):
        return pltpu.make_async_remote_copy(
            src_ref=placed.at[e],
            dst_ref=pix_in.at[1 - ahead, me],
            send_sem=px_send.at[ahead, e],
            recv_sem=px_recv.at[1 - ahead, me],
            device_id=(e, t + ahead),
            device_id_type=MESH,
        )

    for k in range(n_dp):
        e = lax.rem(me + k, n_dp)

        @pl.when(t < n_tm - 1)
        def _():
            pixel_copy(e, 1).start()

        if k:
            pixel_copy(e, 0).start()
    pix_in[1, me] = placed[me]

    @pl.when(t == 0)
    def _():
        pix_in[0] = jnp.zeros(pix_in.shape[1:], BF)
        mid_halo[...] = jnp.zeros(mid_halo.shape, BF)

    place = columns[...]
    weight_in = in_w[...]
    for col in range(PW):
        pick = jnp.where(place == col, 1.0, 0.0).astype(BF)
        toeplitz[:, col * CH : (col + 1) * CH] = jnp.dot(
            pick, weight_in, preferred_element_type=F32
        ).astype(BF)
    for j in range(span + 2):
        act[j, 0] = jnp.zeros((PW, 3 * CH), BF)
        act[j, HS + 1] = jnp.zeros((PW, 3 * CH), BF)
    resid[span * PIX : span * PIX + 16, :] = jnp.zeros((16, CH), F32)

    start = t * span
    ends, begins = [], []
    running = jnp.int32(0)
    for k in range(clips):
        begins.append(running)
        running = running + lengths[k]
        ends.append(running)

    def clip_of(g):
        first, last = begins[0], ends[0]
        for k in range(1, clips):
            later = ends[k - 1] <= g
            first = jnp.where(later, begins[k], first)
            last = jnp.where(later, ends[k], last)
        return first, last

    frame_clip = [clip_of(start - 2 + j) for j in range(span + 2)]

    def picked(j, lag, lead):
        g = start - 2 + j
        return jnp.maximum(g - lag, frame_clip[j][0]) - (start - lead)

    for k in range(1, n_dp):
        d = lax.rem(me + k, n_dp)
        pltpu.make_async_copy(pix_in.at[1, d], pix_in.at[1, d], px_recv.at[1, d]).wait()

    @pl.when(t > 0)
    def _():
        for d in range(n_dp):
            pltpu.make_async_copy(pix_in.at[0, d], pix_in.at[0, d], px_recv.at[0, d]).wait()

    whole = []
    for half in range(2):
        total = pix_in[half, 0].astype(F32)
        for d in range(1, n_dp):
            total = total + pix_in[half, d].astype(F32)
        whole.append(total)
    whole = jnp.concatenate(whole, axis=0)
    lane = lax.broadcasted_iota(jnp.int32, whole.shape, 1)
    for q in range(RB):
        shifted = pltpu.roll(whole, (ROW - q * ROW) % WIDE, axis=1)
        rows = jnp.where((lane >= ROW) & (lane < 2 * ROW), shifted, 0.0)
        for half in range(2):
            pix_rows[half, pl.ds(q, 2 * units, stride=RB), :] = rows[:, half * CH : (half + 1) * CH]
    rows = jnp.concatenate([pix_rows[0], pix_rows[1]], axis=1)
    place = lax.broadcasted_iota(jnp.int32, rows.shape, 0) & (HS - 1)
    count = rows.shape[0]
    above = jnp.where(place == 0, 0.0, pltpu.roll(rows, 1, axis=0))
    below = jnp.where(place == HS - 1, 0.0, pltpu.roll(rows, count - 1, axis=0))
    rows = rows + pltpu.roll(above, WIDE - ROW, axis=1) + pltpu.roll(below, ROW, axis=1)
    xrows[...] = rows.astype(BF).reshape(2 * span, HS, WIDE)

    for j in range(span + 2):
        for kt in range(LAGS):
            lhs[j * HS : (j + 1) * HS, kt * WIDE : (kt + 1) * WIDE] = xrows[picked(j, 2 - kt, 4)]
    patch = lhs[...]
    for col in range(PW):
        part = jnp.dot(
            patch, toeplitz[:, col * CH : (col + 1) * CH], preferred_element_type=F32
        )
        part = (part + vecs[0:1, :]).astype(BF).astype(F32)
        base[pl.ds(col, (span + 2) * HS, stride=PW), :] = part

    def frame_stats(x):
        total = jnp.sum(x, axis=0, keepdims=True)
        away = x - total * (1.0 / PIX)
        return total, jnp.sum(away * away, axis=0, keepdims=True)

    def share_stats(stats, which, rows):
        stats[t] = jnp.concatenate([r[0] for r in rows] + [r[1] for r in rows], axis=0)
        copies = []
        for k in range(1, n_tm):
            other = lax.rem(t + k, n_tm)
            copy = pltpu.make_async_remote_copy(
                src_ref=stats.at[t],
                dst_ref=stats.at[t],
                send_sem=st_send.at[which, k],
                recv_sem=st_recv.at[which, t],
                device_id=(me, other),
                device_id_type=MESH,
            )
            copy.start()
            copies.append(copy)
        return copies

    def norm_terms(stats, which, copies):
        for k in range(1, n_tm):
            other = lax.rem(t + k, n_tm)
            pltpu.make_async_copy(stats.at[other], stats.at[other], st_recv.at[which, other]).wait()
        sums = jnp.concatenate([stats[i, 0:span] for i in range(n_tm)], axis=0)
        devs = jnp.concatenate([stats[i, span : 2 * span] for i in range(n_tm)], axis=0)
        g = lax.broadcasted_iota(jnp.int32, sums.shape, 0)
        share = CH // GROUPS
        inside, sizes, means = [], [], []
        for first, last in frame_clip:
            hit = (g >= first) & (g < last)
            inside.append(hit)
            sizes.append((last - first).astype(F32) * (PIX * share))
            means.append(jnp.sum(jnp.where(hit, sums, 0.0), axis=0, keepdims=True))
        pad = [jnp.zeros((8 - len(means), CH), F32)] if len(means) < 8 else []
        means = group_sum(jnp.concatenate(means + pad, axis=0))
        means = [means[j : j + 1] / sizes[j] for j in range(span + 2)]
        frame_mean = sums * (1.0 / PIX)
        spread = []
        for j in range(span + 2):
            off = frame_mean - means[j]
            spread.append(
                jnp.sum(jnp.where(inside[j], devs + PIX * off * off, 0.0), axis=0, keepdims=True)
            )
        spread = group_sum(jnp.concatenate(spread + pad, axis=0))
        scales = [lax.rsqrt(spread[j : j + 1] / sizes[j] + EPS) for j in range(span + 2)]
        return means, scales

    column = lax.broadcasted_iota(jnp.int32, (PIX, CH), 0) & (PW - 1)

    def activate(j, x, mean, scale, gain, bias):
        y = (x - mean) * (scale * gain) + bias
        y = 0.5 * y
        y = y + y * jnp.tanh(y)
        left = jnp.where(column == 0, 0.0, pltpu.roll(y, 1, axis=0))
        right = jnp.where(column == PW - 1, 0.0, pltpu.roll(y, PIX - 1, axis=0))
        for i, part in enumerate((left, y, right)):
            act[j, 1 : HS + 1, :, i * CH : (i + 1) * CH] = part.astype(BF).reshape(HS, PW, CH)

    def conv_frame(j, weight):
        taps = []
        for kt in range(LAGS):
            p = picked(j, 2 - kt, 2)
            for dy in range(3):
                taps.append(act[p, dy : dy + HS].reshape(PIX, 3 * CH))
        return jnp.dot(jnp.concatenate(taps, axis=1), weight[...], preferred_element_type=F32)

    rows = [frame_stats(base[(j + 2) * PIX : (j + 3) * PIX, :]) for j in range(span)]
    stat_copies = share_stats(stats1, 0, rows)
    means, scales = norm_terms(stats1, 0, stat_copies)
    for j in range(span + 2):
        activate(
            j, base[j * PIX : (j + 1) * PIX, :], means[j], scales[j], vecs[1:2, :], vecs[2:3, :]
        )
    weight_copies[0].wait()

    halo = pltpu.make_async_remote_copy(
        src_ref=mid_send,
        dst_ref=mid_halo,
        send_sem=halo_send,
        recv_sem=halo_recv,
        device_id=(me, t + 1),
        device_id_type=MESH,
    )
    rows = [None] * span
    order = list(range(span - 2, span)) + list(range(span - 2))
    for at, j in enumerate(order):
        x = conv_frame(j + 2, w1).astype(BF)
        if at < 2:
            mid_send[at] = x
        x = x.astype(F32)
        mid[j * PIX : (j + 1) * PIX, :] = x
        rows[j] = frame_stats(x)
        if at == 1:

            @pl.when(t < n_tm - 1)
            def _():
                halo.start()

    stat_copies2 = share_stats(stats2, 1, rows)
    means, scales = norm_terms(stats2, 1, stat_copies2)
    for j in range(span):
        activate(
            j + 2,
            mid[j * PIX : (j + 1) * PIX, :],
            means[j + 2],
            scales[j + 2],
            vecs[3:4, :],
            vecs[4:5, :],
        )

    @pl.when(t > 0)
    def _():
        halo.wait_recv()

    for j in range(2):
        activate(
            j, mid_halo[j].astype(F32), means[j], scales[j], vecs[3:4, :], vecs[4:5, :]
        )
    weight_copies[1].wait()
    for j in range(span):
        x = conv_frame(j + 2, w2) + base[(j + 2) * PIX : (j + 3) * PIX, :]
        resid[j * PIX : (j + 1) * PIX, :] = x.astype(BF).astype(F32)

    weight_copies[2].wait()
    half = PW // 2
    cells = span * HS * half
    spot = lax.broadcasted_iota(jnp.int32, (cells, CH), 0) & (half - 1)
    taps = [None] * 9
    for kx in range(3):
        x = resid[pl.ds(kx, cells, stride=2), :]
        if kx == 2:
            x = jnp.where(spot == half - 1, 0.0, x)
        x = x.reshape(span, HS // 2, 2, half, CH)
        even, odd = x[:, :, 0], x[:, :, 1]
        after = jnp.concatenate(
            [even[:, 1:], jnp.zeros((span, 1, half, CH), F32)], axis=1
        )
        for ky, rows in enumerate((even, odd, after)):
            taps[ky * 3 + kx] = rows.reshape(cells // 2, CH).astype(BF)
    encoded = jnp.dot(jnp.concatenate(taps, axis=1), wd[...], preferred_element_type=F32).astype(BF)
    unit_rows = RB * PW // 4
    latent[0:units] = encoded.reshape(units, unit_rows, CH)
    latent[units:] = jnp.zeros((cap, unit_rows, CH), BF)

    back = []
    for k in range(n_dp):
        d = lax.rem(me + k, n_dp)
        block = latent[pl.ds(recv_start_of(d, me), cap)]
        if k == 0:
            returned[me] = block
        else:
            packed[k] = block
            copy = pltpu.make_async_remote_copy(
                src_ref=packed.at[k],
                dst_ref=returned.at[me],
                send_sem=back_send.at[k],
                recv_sem=back_recv.at[me],
                device_id=(d, t),
                device_id_type=MESH,
            )
            copy.start()
            back.append(copy)
    for k in range(1, n_dp):
        d = lax.rem(me + k, n_dp)
        pltpu.make_async_copy(returned.at[d], returned.at[d], back_recv.at[d]).wait()
    for p in range(units):
        owner = jnp.int32(0)
        first = jnp.int32(0)
        for e in range(1, n_dp):
            later = send_start[e] <= p
            owner = jnp.where(later, e, owner)
            first = jnp.where(later, send_start[e], first)
        gathered[p * unit_rows : (p + 1) * unit_rows, :] = returned[
            owner, jnp.minimum(p - first, cap - 1)
        ].astype(F32)
    for k in range(unit_rows):
        out[:, k * CH : (k + 1) * CH] = gathered[pl.ds(k, units, stride=unit_rows), :].astype(BF)

    for copy in stat_copies + stat_copies2 + back:
        copy.wait_send()
    for k in range(n_dp):
        e = lax.rem(me + k, n_dp)
        if k:
            pixel_copy(e, 0).wait_send()

    @pl.when(t < n_tm - 1)
    def _():
        halo.wait_send()
        for k in range(n_dp):
            pixel_copy(lax.rem(me + k, n_dp), 1).wait_send()


def per_device(
    pixels,
    counts,
    clip_lengths,
    in_weight,
    in_bias,
    norm1_gain,
    norm1_bias,
    conv1_weight,
    norm2_gain,
    norm2_bias,
    conv2_weight,
    down_weight,
):
    n_dp = lax.axis_size("dp")
    n_tm = lax.axis_size("tm")
    units = pixels.shape[2]
    span = units // (HS // RB)
    cap = units // n_dp + 1
    unit_rows = RB * PW // 4
    mine = jnp.pad(pixels[0, 0], ((0, 0), (0, WIDE - pixels.shape[3])))
    in_w = jnp.pad(in_weight.reshape(27 * 3, CH), ((0, CH - 27 * 3), (0, 0)))
    vecs = jnp.stack([in_bias, norm1_gain, norm1_bias, norm2_gain, norm2_bias])
    vmem = pl.BlockSpec(memory_space=pltpu.VMEM)
    smem = pl.BlockSpec(memory_space=pltpu.SMEM)
    hbm = pl.BlockSpec(memory_space=pl.ANY)
    result = pl.pallas_call(
        functools.partial(kernel, n_dp, n_tm),
        out_shape=jax.ShapeDtypeStruct((units, unit_rows * CH), BF),
        in_specs=[smem, smem, vmem, vmem, vmem, vmem, hbm, hbm, hbm],
        out_specs=vmem,
        scratch_shapes=[
            pltpu.VMEM((27 * CH, CH), BF),
            pltpu.VMEM((27 * CH, CH), BF),
            pltpu.VMEM((9 * CH, CH), BF),
            pltpu.VMEM((LAGS * WIDE, PW * CH), BF),
            pltpu.VMEM((n_dp, units, WIDE), BF),
            pltpu.VMEM((2, n_dp, units, WIDE), BF),
            pltpu.VMEM((2, 2 * units * RB, CH), F32),
            pltpu.VMEM((2 * span, HS, WIDE), BF),
            pltpu.VMEM(((span + 2) * HS, LAGS * WIDE), BF),
            pltpu.VMEM(((span + 2) * PIX, CH), F32),
            pltpu.VMEM((span * PIX, CH), F32),
            pltpu.VMEM((span + 2, HS + 2, PW, 3 * CH), BF),
            pltpu.VMEM((span * PIX + 16, CH), F32),
            pltpu.VMEM((2, PIX, CH), BF),
            pltpu.VMEM((2, PIX, CH), BF),
            pltpu.VMEM((n_tm, 2 * span, CH), F32),
            pltpu.VMEM((n_tm, 2 * span, CH), F32),
            pltpu.VMEM((units + cap, unit_rows, CH), BF),
            pltpu.VMEM((n_dp, cap, unit_rows, CH), BF),
            pltpu.VMEM((n_dp, cap, unit_rows, CH), BF),
            pltpu.VMEM((units * unit_rows, CH), F32),
            pltpu.SemaphoreType.DMA((3,)),
            pltpu.SemaphoreType.DMA((2, n_dp)),
            pltpu.SemaphoreType.DMA((2, n_dp)),
            pltpu.SemaphoreType.DMA((2, n_tm)),
            pltpu.SemaphoreType.DMA((2, n_tm)),
            pltpu.SemaphoreType.DMA(()),
            pltpu.SemaphoreType.DMA(()),
            pltpu.SemaphoreType.DMA((n_dp,)),
            pltpu.SemaphoreType.DMA((n_dp,)),
        ],
        compiler_params=pltpu.CompilerParams(
            collective_id=0, has_side_effects=True, vmem_limit_bytes=48 * 1024 * 1024
        ),
        name="encoder_block",
    )(
        counts[0],
        clip_lengths[0],
        mine,
        jnp.asarray(tap_columns()),
        in_w,
        vecs,
        conv1_weight.reshape(27 * CH, CH),
        conv2_weight.reshape(27 * CH, CH),
        down_weight.reshape(9 * CH, CH),
    )
    return result.reshape(1, 1, units, unit_rows * CH)


def solution(mesh):
    in_specs = (
        P("dp", "tm", None, None),
        P("tm", None, None),
        P("dp", None),
        P(),
        P(),
        P(),
        P(),
        P(),
        P(),
        P(),
        P(),
        P(),
    )
    out_specs = P("dp", "tm", None, None)
    return jax.shard_map(
        per_device, mesh=mesh, in_specs=in_specs, out_specs=out_specs, check_vma=False
    )
```

profile of v0, /device:TPU:0, one launch (start us, length us, event | category | flops | bytes accessed | tf_op | source)
XLA Modules:
  0.0 42.3 jit_solution(6347222302630143064)
XLA Ops:
  0.0 0.0 copy-start.7
  0.0 0.0 copy-start.8
  0.0 0.0 copy-start.9
  0.0 0.0 copy-start.10
  0.0 0.0 copy-start.11
  0.0 0.0 copy-start.12
  0.0 0.0 copy-start.6
  0.0 0.6 %copy-done.8 = f32[128]{0:T(128)S(1)} copy-done((f32[128]{0:T(128)S(1)}, f32[128]{0:T(128)}, u32[]{:S(2)}) %copy-start.8) | copy-done | bytes 536
  0.7 0.0 copy-done.9
  0.7 0.0 copy-done.10
  0.7 0.0 copy-done.11
  0.7 0.0 copy-done.12
  0.8 0.0 copy-done.7
  0.8 0.0 copy-done.6
  0.9 0.0 copy-start.4
  0.9 0.0 copy-start.5
  0.9 0.6 %copy-done.4 = s32[1,4,4]{2,1,0:T(4,128)S(1)} copy-done((s32[1,4,4]{2,1,0:T(4,128)S(1)}, s32[1,4,4]{2,1,0:T(4,128)}, u32[]{:S(2)}) %copy-start.4) | copy-done | bytes 88
  1.6 0.0 copy-done.5
  1.6 0.0 copy-start
  1.6 1.2 %copy-done = bf16[3,3,3,128,128]{4,3,2,1,0:T(8,128)(2,1)S(1)} copy-done((bf16[3,3,3,128,128]{4,3,2,1,0:T(8,128)(2,1)S(1)}, bf16[3,3,3,128,128]{4,3,2,1,0:T(8,128)(2,1)}, u32[]{:S(2)}) %copy-start) | copy-done | bytes 884760
  2.7 0.0 copy-start.1
  2.7 1.2 %copy-done.1 = bf16[3,3,3,128,128]{4,3,2,1,0:T(8,128)(2,1)S(1)} copy-done((bf16[3,3,3,128,128]{4,3,2,1,0:T(8,128)(2,1)S(1)}, bf16[3,3,3,128,128]{4,3,2,1,0:T(8,128)(2,1)}, u32[]{:S(2)}) %copy-start.1) | copy-done | bytes 884760
  3.9 0.0 copy-start.2
  3.9 1.0 %copy-done.2 = s32[768,128]{1,0:T(8,128)S(1)} copy-done((s32[768,128]{1,0:T(8,128)S(1)}, s32[768,128]{1,0:T(8,128)}, u32[]{:S(2)}) %copy-start.2) | copy-done | bytes 393240
  4.9 0.0 copy-start.3
  4.9 1.0 %copy-done.3 = bf16[3,3,128,128]{3,2,1,0:T(8,128)(2,1)S(1)} copy-done((bf16[3,3,128,128]{3,2,1,0:T(8,128)(2,1)S(1)}, bf16[3,3,128,128]{3,2,1,0:T(8,128)(2,1)}, u32[]{:S(2)}) %copy-start.3) | copy-done | bytes 294936
  5.8 35.7 %encoder_block.1 = bf16[32,2048]{1,0:T(8,128)(2,1)S(1)} custom-call(s32[4,4]{1,0:T(4,128)S(1)} %bitcast.16, s32[4]{0:T(128)S(1)} %bitcast.17, bf16[32,256]{1,0:T(8,128)(2,1)S(1)} %pad.8.pixels, s32[768,128]{1,0:T(8,128)S(1)} %copy-done.2, bf16[128,128]{1,0:T(8,128)(2,1)S(1)} %pad.9.in_w, f32[5,128]{1,0:T(8,128)S(1)} %stack.23.vecs, ...), custom_call_target="tpu_custom_call" | custom-call | tf_op jit(solution)/shard_map/encoder_block/pallas_call | solution.py:480
  41.6 0.7 %copy.15 = bf16[1,1,32,2048]{3,2,1,0:T(8,128)(2,1)} copy(bf16[1,1,32,2048]{3,2,1,0:T(8,128)(2,1)S(1)} %bitcast.14) | data formatting | bytes 262144
  (4 shorter events, 0.1 us)
Async XLA Ops:
  0.0 0.8 %copy-start.7 = (bf16[1,1,32,192]{3,2,1,0:T(8,128)(2,1)S(1)}, bf16[1,1,32,192]{3,2,1,0:T(8,128)(2,1)}, u32[]{:S(2)}) copy-start(bf16[1,1,32,192]{3,2,1,0:T(8,128)(2,1)} %param.13) | copy-start | bytes 36868
  0.0 0.7 %copy-start.8 = (f32[128]{0:T(128)S(1)}, f32[128]{0:T(128)}, u32[]{:S(2)}) copy-start(f32[128]{0:T(128)} %param.17) | copy-start | bytes 1540
  0.0 0.7 %copy-start.9 = (f32[128]{0:T(128)S(1)}, f32[128]{0:T(128)}, u32[]{:S(2)}) copy-start(f32[128]{0:T(128)} %param.18) | copy-start | bytes 1540
  0.0 0.7 %copy-start.10 = (f32[128]{0:T(128)S(1)}, f32[128]{0:T(128)}, u32[]{:S(2)}) copy-start(f32[128]{0:T(128)} %param.19) | copy-start | bytes 1540
  0.0 0.7 %copy-start.11 = (f32[128]{0:T(128)S(1)}, f32[128]{0:T(128)}, u32[]{:S(2)}) copy-start(f32[128]{0:T(128)} %param.21) | copy-start | bytes 1540
  0.0 0.7 %copy-start.12 = (f32[128]{0:T(128)S(1)}, f32[128]{0:T(128)}, u32[]{:S(2)}) copy-start(f32[128]{0:T(128)} %param.22) | copy-start | bytes 1540
  0.0 0.8 %copy-start.6 = (bf16[3,3,3,3,128]{4,3,2,1,0:T(4,128)(2,1)S(1)}, bf16[3,3,3,3,128]{4,3,2,1,0:T(4,128)(2,1)}, u32[]{:S(2)}) copy-start(bf16[3,3,3,3,128]{4,3,2,1,0:T(4,128)(2,1)} %param.16) | copy-start | bytes 62212
  0.9 0.7 %copy-start.4 = (s32[1,4,4]{2,1,0:T(4,128)S(1)}, s32[1,4,4]{2,1,0:T(4,128)}, u32[]{:S(2)}) copy-start(s32[1,4,4]{2,1,0:T(4,128)} %param.14) | copy-start | bytes 196
  0.9 0.7 %copy-start.5 = (s32[1,4]{1,0:T(1,128)S(1)}, s32[1,4]{1,0:T(1,128)}, u32[]{:S(2)}) copy-start(s32[1,4]{1,0:T(1,128)} %param.15) | copy-start | bytes 52
  1.6 1.2 %copy-start = (bf16[3,3,3,128,128]{4,3,2,1,0:T(8,128)(2,1)S(1)}, bf16[3,3,3,128,128]{4,3,2,1,0:T(8,128)(2,1)}, u32[]{:S(2)}) copy-start(bf16[3,3,3,128,128]{4,3,2,1,0:T(8,128)(2,1)} %param.20) | copy-start | bytes 2654212
  2.7 1.2 %copy-start.1 = (bf16[3,3,3,128,128]{4,3,2,1,0:T(8,128)(2,1)S(1)}, bf16[3,3,3,128,128]{4,3,2,1,0:T(8,128)(2,1)}, u32[]{:S(2)}) copy-start(bf16[3,3,3,128,128]{4,3,2,1,0:T(8,128)(2,1)} %param.23) | copy-start | bytes 2654212
  3.9 1.0 %copy-start.2 = (s32[768,128]{1,0:T(8,128)S(1)}, s32[768,128]{1,0:T(8,128)}, u32[]{:S(2)}) copy-start(s32[768,128]{1,0:T(8,128)} %constant.5.clone.columns) | copy-start | bytes 1179652
  4.9 1.0 %copy-start.3 = (bf16[3,3,128,128]{3,2,1,0:T(8,128)(2,1)S(1)}, bf16[3,3,128,128]{3,2,1,0:T(8,128)(2,1)}, u32[]{:S(2)}) copy-start(bf16[3,3,128,128]{3,2,1,0:T(8,128)(2,1)} %param.24) | copy-start | bytes 884740
where the time goes:
time: 42.6 us; the launch traced here: 42.3 us
  Pallas kernels  35.7 us (84%)
  local copies, waits for them, and re-layouts  6.45 us (15%)
    pallas_call x1, Pallas kernels, per_device(): pl.pallas_call(functools.partial(kernel, n_dp, n_tm), out_shape=jax.Shape...  35.7 us
    unnamed x27, local copies, waits for them, and re-layouts  6.39 us

commit v1 on v0

--- a/solution.py
+++ b/solution.py
@@ -21,6 +21,9 @@
 WIDE = 256
 ROW = PW * 3
 PIX = HS * PW
+HALF = PIX // 2
+PAIRS = PW // 2
+PART = 64
 
 
 def tap_columns():
@@ -31,7 +34,7 @@
                 for color in range(3):
                     r = kt * WIDE + dy * ROW + col * 3 + color
                     for dx in range(3):
-                        table[r, ((kt * 3 + dy) * 3 + dx) * 3 + color] = col + 1 - dx
+                        table[r, ((kt * 3 + dy) * 3 + dx) * 4 + color] = col + 1 - dx
     return table
 
 
@@ -47,16 +50,27 @@
 def kernel(
     n_dp,
     n_tm,
+    counts_hbm,
+    lengths_hbm,
+    pixels_hbm,
+    columns_hbm,
+    in_w_hbm,
+    bias0_hbm,
+    gain1_hbm,
+    bias1_hbm,
+    gain2_hbm,
+    bias2_hbm,
+    w1_hbm,
+    w2_hbm,
+    wd_hbm,
+    out,
     counts,
     lengths,
     pixels,
     columns,
     in_w,
     vecs,
-    w1_hbm,
-    w2_hbm,
-    wd_hbm,
-    out,
+    taps_w,
     w1,
     w2,
     wd,
@@ -68,7 +82,8 @@
     lhs,
     base,
     mid,
-    act,
+    act_a,
+    act_b,
     resid,
     mid_send,
     mid_halo,
@@ -78,6 +93,7 @@
     packed,
     returned,
     gathered,
+    small_sem,
     w_sem,
     px_send,
     px_recv,
@@ -94,7 +110,7 @@
     cap = units // n_dp + 1
     me = lax.axis_index("dp")
     t = lax.axis_index("tm")
-    clips = lengths.shape[0]
+    clips = lengths.shape[1]
 
     barrier = pltpu.get_barrier_semaphore()
 
@@ -115,12 +131,38 @@
         def _():
             greet(d, t + 1)
 
+    small = (
+        (pixels_hbm.at[0, 0], pixels),
+        (counts_hbm.at[0], counts),
+        (columns_hbm, columns),
+        (in_w_hbm, in_w),
+        (lengths_hbm, lengths),
+        (bias0_hbm, vecs.at[0]),
+        (gain1_hbm, vecs.at[1]),
+        (bias1_hbm, vecs.at[2]),
+        (gain2_hbm, vecs.at[3]),
+        (bias2_hbm, vecs.at[4]),
+    )
+    small_copies = [
+        pltpu.make_async_copy(src, dst, small_sem.at[i]) for i, (src, dst) in enumerate(small)
+    ]
+    for copy in small_copies:
+        copy.start()
+    side = 3 * CH
+    large = (
+        (w1_hbm, w1.at[:, 0:side, 0:CH]),
+        (w1_hbm, w1.at[:, CH : CH + side, CH : 2 * CH]),
+        (w2_hbm, w2.at[:, 0:side, 0:CH]),
+        (w2_hbm, w2.at[:, CH : CH + side, CH : 2 * CH]),
+        (wd_hbm, wd),
+    )
     weight_copies = [
-        pltpu.make_async_copy(src, dst, w_sem.at[i])
-        for i, (src, dst) in enumerate(((w1_hbm, w1), (w2_hbm, w2), (wd_hbm, wd)))
+        pltpu.make_async_copy(src, dst, w_sem.at[i]) for i, (src, dst) in enumerate(large)
     ]
     for copy in weight_copies:
         copy.start()
+    small_copies[0].wait()
+    small_copies[1].wait()
 
     def recv_start_of(d, e):
         total = jnp.int32(0)
@@ -141,7 +183,7 @@
     for e in range(n_dp):
         turn = recv_start_of(me, e) - send_start[e]
         hit = (place_r == place_i + turn) & (place_i >= send_start[e]) & (place_i < send_end[e])
-        placed[e] = jnp.dot(
+        placed[e, :, 0 : RB * ROW] = jnp.dot(
             hit.astype(F32).astype(BF), mine, preferred_element_type=F32
         ).astype(BF)
 
@@ -181,24 +223,29 @@
         pix_in[0] = jnp.zeros(pix_in.shape[1:], BF)
         mid_halo[...] = jnp.zeros(mid_halo.shape, BF)
 
+    for copy in small_copies[2:]:
+        copy.wait()
+    taps_w[...] = jnp.zeros(taps_w.shape, F32)
+    for tap in range(27):
+        kt, dy, dx = tap // 9, tap // 3 % 3, tap % 3
+        taps_w[4 * tap : 4 * tap + 3, :] = in_w[kt, dy, dx].astype(F32)
     place = columns[...]
-    weight_in = in_w[...]
+    weight_in = taps_w[...].astype(BF)
     for col in range(PW):
         pick = jnp.where(place == col, 1.0, 0.0).astype(BF)
         toeplitz[:, col * CH : (col + 1) * CH] = jnp.dot(
             pick, weight_in, preferred_element_type=F32
         ).astype(BF)
-    for j in range(span + 2):
-        act[j, 0] = jnp.zeros((PW, 3 * CH), BF)
-        act[j, HS + 1] = jnp.zeros((PW, 3 * CH), BF)
-    resid[span * PIX : span * PIX + 16, :] = jnp.zeros((16, CH), F32)
+    for weight in (w1, w2):
+        weight[:, side : side + CH, 0:CH] = jnp.zeros((9, CH, CH), BF)
+        weight[:, 0:CH, CH : 2 * CH] = jnp.zeros((9, CH, CH), BF)
 
     start = t * span
     ends, begins = [], []
     running = jnp.int32(0)
     for k in range(clips):
         begins.append(running)
-        running = running + lengths[k]
+        running = running + lengths[0, k]
         ends.append(running)
 
     def clip_of(g):
@@ -249,17 +296,20 @@
         for kt in range(LAGS):
             lhs[j * HS : (j + 1) * HS, kt * WIDE : (kt + 1) * WIDE] = xrows[picked(j, 2 - kt, 4)]
     patch = lhs[...]
-    for col in range(PW):
-        part = jnp.dot(
-            patch, toeplitz[:, col * CH : (col + 1) * CH], preferred_element_type=F32
+    for pair in range(PAIRS):
+        both = jnp.dot(
+            patch, toeplitz[:, pair * 2 * CH : (pair + 1) * 2 * CH], preferred_element_type=F32
         )
-        part = (part + vecs[0:1, :]).astype(BF).astype(F32)
-        base[pl.ds(col, (span + 2) * HS, stride=PW), :] = part
-
-    def frame_stats(x):
-        total = jnp.sum(x, axis=0, keepdims=True)
-        away = x - total * (1.0 / PIX)
-        return total, jnp.sum(away * away, axis=0, keepdims=True)
+        for side_at in range(2):
+            part = both[:, side_at * CH : (side_at + 1) * CH] + vecs[0]
+            base[side_at, pl.ds(pair, (span + 2) * HS, stride=PAIRS), :] = part.astype(BF).astype(F32)
+
+    def frame_stats(even, odd):
+        total = jnp.sum(even, axis=0, keepdims=True) + jnp.sum(odd, axis=0, keepdims=True)
+        mean = total * (1.0 / PIX)
+        even, odd = even - mean, odd - mean
+        away = jnp.sum(even * even, axis=0, keepdims=True) + jnp.sum(odd * odd, axis=0, keepdims=True)
+        return total, away
 
     def share_stats(stats, which, rows):
         stats[t] = jnp.concatenate([r[0] for r in rows] + [r[1] for r in rows], axis=0)
@@ -306,33 +356,56 @@
         scales = [lax.rsqrt(spread[j : j + 1] / sizes[j] + EPS) for j in range(span + 2)]
         return means, scales
 
-    column = lax.broadcasted_iota(jnp.int32, (PIX, CH), 0) & (PW - 1)
-
-    def activate(j, x, mean, scale, gain, bias):
-        y = (x - mean) * (scale * gain) + bias
-        y = 0.5 * y
-        y = y + y * jnp.tanh(y)
-        left = jnp.where(column == 0, 0.0, pltpu.roll(y, 1, axis=0))
-        right = jnp.where(column == PW - 1, 0.0, pltpu.roll(y, PIX - 1, axis=0))
-        for i, part in enumerate((left, y, right)):
-            act[j, 1 : HS + 1, :, i * CH : (i + 1) * CH] = part.astype(BF).reshape(HS, PW, CH)
+    pair_at = lax.broadcasted_iota(jnp.int32, (PART, CH), 0) & (PAIRS - 1)
+    blank = jnp.zeros((PAIRS, CH), F32)
+
+    def activate(j, source, first, mean, scale, gain, bias):
+        factor = scale * gain
+        carry = [blank] * 4
+        for at in range(0, HALF, PART):
+            done = []
+            for side_at in range(2):
+                x = source(side_at, first + at)
+                y = 0.5 * ((x - mean) * factor + bias)
+                done.append(y + y * jnp.tanh(y))
+            even, odd = done
+            before = jnp.where(pair_at == 0, 0.0, pltpu.roll(odd, 1, axis=0))
+            after = jnp.where(pair_at == PAIRS - 1, 0.0, pltpu.roll(even, PART - 1, axis=0))
+            for i, part in enumerate((before, even, odd, after)):
+                lanes = slice(i * CH, (i + 1) * CH)
+                act_b[j, at : at + PART, lanes] = part.astype(BF)
+                late = jnp.concatenate([carry[i], part[: PART - PAIRS]], axis=0)
+                act_a[j, at : at + PART, lanes] = late.astype(BF)
+                carry[i] = part[PART - PAIRS :]
+        for i in range(4):
+            act_a[j, HALF : HALF + 2 * PAIRS, i * CH : (i + 1) * CH] = jnp.concatenate(
+                [carry[i], blank], axis=0
+            ).astype(BF)
 
     def conv_frame(j, weight):
         taps = []
         for kt in range(LAGS):
             p = picked(j, 2 - kt, 2)
-            for dy in range(3):
-                taps.append(act[p, dy : dy + HS].reshape(PIX, 3 * CH))
-        return jnp.dot(jnp.concatenate(taps, axis=1), weight[...], preferred_element_type=F32)
-
-    rows = [frame_stats(base[(j + 2) * PIX : (j + 3) * PIX, :]) for j in range(span)]
+            taps += [act_a[p, 0:HALF], act_b[p], act_a[p, 2 * PAIRS : 2 * PAIRS + HALF]]
+        both = jnp.dot(
+            jnp.concatenate(taps, axis=1),
+            weight[...].reshape(9 * 4 * CH, 2 * CH),
+            preferred_element_type=F32,
+        )
+        return both[:, :CH], both[:, CH:]
+
+    rows = [
+        frame_stats(*[base[i, (j + 2) * HALF : (j + 3) * HALF, :] for i in range(2)])
+        for j in range(span)
+    ]
     stat_copies = share_stats(stats1, 0, rows)
     means, scales = norm_terms(stats1, 0, stat_copies)
     for j in range(span + 2):
         activate(
-            j, base[j * PIX : (j + 1) * PIX, :], means[j], scales[j], vecs[1:2, :], vecs[2:3, :]
+            j, lambda i, at: base[i, at : at + PART, :], j * HALF, means[j], scales[j], vecs[1], vecs[2]
         )
     weight_copies[0].wait()
+    weight_copies[1].wait()
 
     halo = pltpu.make_async_remote_copy(
         src_ref=mid_send,
@@ -345,12 +418,15 @@
     rows = [None] * span
     order = list(range(span - 2, span)) + list(range(span - 2))
     for at, j in enumerate(order):
-        x = conv_frame(j + 2, w1).astype(BF)
-        if at < 2:
-            mid_send[at] = x
-        x = x.astype(F32)
-        mid[j * PIX : (j + 1) * PIX, :] = x
-        rows[j] = frame_stats(x)
+        pieces = []
+        for i, x in enumerate(conv_frame(j + 2, w1)):
+            x = x.astype(BF)
+            if at < 2:
+                mid_send[at, i] = x
+            x = x.astype(F32)
+            mid[i, j * HALF : (j + 1) * HALF, :] = x
+            pieces.append(x)
+        rows[j] = frame_stats(*pieces)
         if at == 1:
 
             @pl.when(t < n_tm - 1)
@@ -362,11 +438,12 @@
     for j in range(span):
         activate(
             j + 2,
-            mid[j * PIX : (j + 1) * PIX, :],
+            lambda i, at: mid[i, at : at + PART, :],
+            j * HALF,
             means[j + 2],
             scales[j + 2],
-            vecs[3:4, :],
-            vecs[4:5, :],
+            vecs[3],
+            vecs[4],
         )
 
     @pl.when(t > 0)
@@ -375,28 +452,32 @@
 
     for j in range(2):
         activate(
-            j, mid_halo[j].astype(F32), means[j], scales[j], vecs[3:4, :], vecs[4:5, :]
+            j,
+            lambda i, at: mid_halo[j, i, at : at + PART, :].astype(F32),
+            0,
+            means[j],
+            scales[j],
+            vecs[3],
+            vecs[4],
         )
-    weight_copies[1].wait()
+    weight_copies[2].wait()
+    weight_copies[3].wait()
     for j in range(span):
-        x = conv_frame(j + 2, w2) + base[(j + 2) * PIX : (j + 3) * PIX, :]
-        resid[j * PIX : (j + 1) * PIX, :] = x.astype(BF).astype(F32)
-
-    weight_copies[2].wait()
-    half = PW // 2
-    cells = span * HS * half
-    spot = lax.broadcasted_iota(jnp.int32, (cells, CH), 0) & (half - 1)
+        for i, x in enumerate(conv_frame(j + 2, w2)):
+            x = x + base[i, (j + 2) * HALF : (j + 3) * HALF, :]
+            resid[i, j * HALF : (j + 1) * HALF, :] = x.astype(BF).astype(F32)
+
+    weight_copies[4].wait()
+    cells = span * HALF
+    spot = lax.broadcasted_iota(jnp.int32, (cells, CH), 0) & (PAIRS - 1)
     taps = [None] * 9
-    for kx in range(3):
-        x = resid[pl.ds(kx, cells, stride=2), :]
-        if kx == 2:
-            x = jnp.where(spot == half - 1, 0.0, x)
-        x = x.reshape(span, HS // 2, 2, half, CH)
-        even, odd = x[:, :, 0], x[:, :, 1]
-        after = jnp.concatenate(
-            [even[:, 1:], jnp.zeros((span, 1, half, CH), F32)], axis=1
-        )
-        for ky, rows in enumerate((even, odd, after)):
+    even, odd = resid[0], resid[1]
+    next_even = jnp.where(spot == PAIRS - 1, 0.0, pltpu.roll(even, cells - 1, axis=0))
+    for kx, x in enumerate((even, odd, next_even)):
+        x = x.reshape(span, HS // 2, 2, PAIRS, CH)
+        upper, lower = x[:, :, 0], x[:, :, 1]
+        below = jnp.concatenate([upper[:, 1:], jnp.zeros((span, 1, PAIRS, CH), F32)], axis=1)
+        for ky, rows in enumerate((upper, lower, below)):
             taps[ky * 3 + kx] = rows.reshape(cells // 2, CH).astype(BF)
     encoded = jnp.dot(jnp.concatenate(taps, axis=1), wd[...], preferred_element_type=F32).astype(BF)
     unit_rows = RB * PW // 4
@@ -471,20 +552,23 @@
     span = units // (HS // RB)
     cap = units // n_dp + 1
     unit_rows = RB * PW // 4
-    mine = jnp.pad(pixels[0, 0], ((0, 0), (0, WIDE - pixels.shape[3])))
-    in_w = jnp.pad(in_weight.reshape(27 * 3, CH), ((0, CH - 27 * 3), (0, 0)))
-    vecs = jnp.stack([in_bias, norm1_gain, norm1_bias, norm2_gain, norm2_bias])
     vmem = pl.BlockSpec(memory_space=pltpu.VMEM)
-    smem = pl.BlockSpec(memory_space=pltpu.SMEM)
-    hbm = pl.BlockSpec(memory_space=pl.ANY)
+    hbm = pl.BlockSpec(memory_space=pltpu.MemorySpace.HBM)
     result = pl.pallas_call(
         functools.partial(kernel, n_dp, n_tm),
         out_shape=jax.ShapeDtypeStruct((units, unit_rows * CH), BF),
-        in_specs=[smem, smem, vmem, vmem, vmem, vmem, hbm, hbm, hbm],
+        in_specs=[hbm] * 13,
         out_specs=vmem,
         scratch_shapes=[
-            pltpu.VMEM((27 * CH, CH), BF),
-            pltpu.VMEM((27 * CH, CH), BF),
+            pltpu.SMEM((n_dp, n_dp), jnp.int32),
+            pltpu.SMEM(clip_lengths.shape, jnp.int32),
+            pltpu.VMEM(pixels.shape[2:], BF),
+            pltpu.VMEM((LAGS * WIDE, CH), jnp.int32),
+            pltpu.VMEM(in_weight.shape, BF),
+            pltpu.VMEM((5, 1, CH), F32),
+            pltpu.VMEM((CH, CH), F32),
+            pltpu.VMEM((9, 4 * CH, 2 * CH), BF),
+            pltpu.VMEM((9, 4 * CH, 2 * CH), BF),
             pltpu.VMEM((9 * CH, CH), BF),
             pltpu.VMEM((LAGS * WIDE, PW * CH), BF),
             pltpu.VMEM((n_dp, units, WIDE), BF),
@@ -492,19 +576,21 @@
             pltpu.VMEM((2, 2 * units * RB, CH), F32),
             pltpu.VMEM((2 * span, HS, WIDE), BF),
             pltpu.VMEM(((span + 2) * HS, LAGS * WIDE), BF),
-            pltpu.VMEM(((span + 2) * PIX, CH), F32),
-            pltpu.VMEM((span * PIX, CH), F32),
-            pltpu.VMEM((span + 2, HS + 2, PW, 3 * CH), BF),
-            pltpu.VMEM((span * PIX + 16, CH), F32),
-            pltpu.VMEM((2, PIX, CH), BF),
-            pltpu.VMEM((2, PIX, CH), BF),
+            pltpu.VMEM((2, (span + 2) * HALF, CH), F32),
+            pltpu.VMEM((2, span * HALF, CH), F32),
+            pltpu.VMEM((span + 2, HALF + 2 * PAIRS, 4 * CH), BF),
+            pltpu.VMEM((span + 2, HALF, 4 * CH), BF),
+            pltpu.VMEM((2, span * HALF, CH), F32),
+            pltpu.VMEM((2, 2, HALF, CH), BF),
+            pltpu.VMEM((2, 2, HALF, CH), BF),
             pltpu.VMEM((n_tm, 2 * span, CH), F32),
             pltpu.VMEM((n_tm, 2 * span, CH), F32),
             pltpu.VMEM((units + cap, unit_rows, CH), BF),
             pltpu.VMEM((n_dp, cap, unit_rows, CH), BF),
             pltpu.VMEM((n_dp, cap, unit_rows, CH), BF),
             pltpu.VMEM((units * unit_rows, CH), F32),
-            pltpu.SemaphoreType.DMA((3,)),
+            pltpu.SemaphoreType.DMA((10,)),
+            pltpu.SemaphoreType.DMA((5,)),
             pltpu.SemaphoreType.DMA((2, n_dp)),
             pltpu.SemaphoreType.DMA((2, n_dp)),
             pltpu.SemaphoreType.DMA((2, n_tm)),
@@ -519,14 +605,14 @@
         ),
         name="encoder_block",
     )(
-        counts[0],
-        clip_lengths[0],
-        mine,
+        counts,
+        clip_lengths,
+        pixels,
         jnp.asarray(tap_columns()),
-        in_w,
-        vecs,
-        conv1_weight.reshape(27 * CH, CH),
-        conv2_weight.reshape(27 * CH, CH),
+        in_weight,
+        *[v.reshape(1, CH) for v in (in_bias, norm1_gain, norm1_bias, norm2_gain, norm2_bias)],
+        conv1_weight.reshape(9, 3 * CH, CH),
+        conv2_weight.reshape(9, 3 * CH, CH),
         down_weight.reshape(9 * CH, CH),
     )
     return result.reshape(1, 1, units, unit_rows * CH)

time: 42.6 us -> 38.2 us (0.90)
  Pallas kernels: 35.7 us -> 30.6 us
  local copies, waits for them, and re-layouts: 6.45 us -> 7.13 us
    pallas_call x1, Pallas kernels: 35.7 us -> 30.6 us  [per_device(): pl.pallas_call(functools.partial(kernel, n_dp, n_tm), out_shape=jax.Shape...]
    unnamed x27, local copies, waits for them, and re-layouts: 6.39 us -> 7.13 us
where the time goes in v1:
time: 38.2 us; the launch traced here: 37.8 us
  Pallas kernels  30.6 us (80%)
  local copies, waits for them, and re-layouts  7.13 us (19%)
    pallas_call x1, Pallas kernels, per_device(): pl.pallas_call(functools.partial(kernel, n_dp, n_tm), out_shape=jax.Shape...  30.6 us
    unnamed x27, local copies, waits for them, and re-layouts  7.13 us

profile of v1, /device:TPU:0, one launch (start us, length us, event | category | flops | bytes accessed | tf_op | source)
XLA Modules:
  0.0 37.8 jit_solution(3729717172209739606)
XLA Ops:
  0.0 0.0 copy-start.10
  0.0 0.0 copy-start.11
  0.0 0.0 copy-start.12
  0.0 0.0 copy-start.6
  0.0 0.0 copy-start.7
  0.0 0.0 copy-start.8
  0.0 0.0 copy-start.9
  0.0 0.6 %copy-done.10 = f32[128]{0:T(128)S(1)} copy-done((f32[128]{0:T(128)S(1)}, f32[128]{0:T(128)}, u32[]{:S(2)}) %copy-start.10) | copy-done | bytes 536
  0.7 0.0 copy-done.11
  0.7 0.0 copy-done.12
  0.7 0.0 copy-done.6
  0.7 0.0 copy-done.7
  0.7 0.0 copy-done.8
  0.7 0.0 copy-done.9
  0.8 0.0 copy-start
  0.8 1.2 %copy-done = bf16[3,3,3,128,128]{4,3,2,1,0:T(8,128)(2,1)S(1)} copy-done((bf16[3,3,3,128,128]{4,3,2,1,0:T(8,128)(2,1)S(1)}, bf16[3,3,3,128,128]{4,3,2,1,0:T(8,128)(2,1)}, u32[]{:S(2)}) %copy-start) | copy-done | bytes 884760
  1.9 0.0 copy-start.1
  1.9 1.2 %copy-done.1 = bf16[3,3,3,128,128]{4,3,2,1,0:T(8,128)(2,1)S(1)} copy-done((bf16[3,3,3,128,128]{4,3,2,1,0:T(8,128)(2,1)S(1)}, bf16[3,3,3,128,128]{4,3,2,1,0:T(8,128)(2,1)}, u32[]{:S(2)}) %copy-start.1) | copy-done | bytes 884760
  3.1 0.0 copy-start.2
  3.1 1.0 %copy-done.2 = s32[768,128]{1,0:T(8,128)S(1)} copy-done((s32[768,128]{1,0:T(8,128)S(1)}, s32[768,128]{1,0:T(8,128)}, u32[]{:S(2)}) %copy-start.2) | copy-done | bytes 393240
  4.1 0.0 copy-start.3
  4.1 1.0 %copy-done.3 = bf16[3,3,128,128]{3,2,1,0:T(8,128)(2,1)S(1)} copy-done((bf16[3,3,128,128]{3,2,1,0:T(8,128)(2,1)S(1)}, bf16[3,3,128,128]{3,2,1,0:T(8,128)(2,1)}, u32[]{:S(2)}) %copy-start.3) | copy-done | bytes 294936
  5.0 0.0 copy-start.4
  5.0 0.7 %copy-done.4 = bf16[3,3,3,3,128]{4,3,2,1,0:T(4,128)(2,1)S(1)} copy-done((bf16[3,3,3,3,128]{4,3,2,1,0:T(4,128)(2,1)S(1)}, bf16[3,3,3,3,128]{4,3,2,1,0:T(4,128)(2,1)}, u32[]{:S(2)}) %copy-start.4) | copy-done | bytes 20760
  5.8 0.0 copy-start.5
  5.8 0.7 %copy-done.5 = bf16[1,1,32,192]{3,2,1,0:T(8,128)(2,1)S(1)} copy-done((bf16[1,1,32,192]{3,2,1,0:T(8,128)(2,1)S(1)}, bf16[1,1,32,192]{3,2,1,0:T(8,128)(2,1)}, u32[]{:S(2)}) %copy-start.5) | copy-done | bytes 12312
  6.5 30.6 %encoder_block.1 = bf16[32,2048]{1,0:T(8,128)(2,1)S(1)} custom-call(s32[1,4,4]{2,1,0:T(4,128)S(1)} %copy-done.6, s32[1,4]{1,0:T(1,128)S(1)} %copy-done.7, bf16[1,1,32,192]{3,2,1,0:T(8,128)(2,1)S(1)} %copy-done.5, s32[768,128]{1,0:T(8,128)S(1)} %copy-done.2, bf16[3,3,3,3,128]{4,3,2,1,0:T(4,128)(2,1)S(1)} %copy-done.4, f32[1,128]{1,0:T(1,128)S(1)} %bitcast.13, ...), custom_call_target="tpu_custom_call" | custom-call | tf_op jit(solution)/shard_map/encoder_block/pallas_call | solution.py:557
  37.1 0.7 %copy.15 = bf16[1,1,32,2048]{3,2,1,0:T(8,128)(2,1)} copy(bf16[1,1,32,2048]{3,2,1,0:T(8,128)(2,1)S(1)} %bitcast.11) | data formatting | bytes 262144
Async XLA Ops:
  0.0 0.7 %copy-start.10 = (f32[128]{0:T(128)S(1)}, f32[128]{0:T(128)}, u32[]{:S(2)}) copy-start(f32[128]{0:T(128)} %param.19) | copy-start | bytes 1540
  0.0 0.7 %copy-start.11 = (f32[128]{0:T(128)S(1)}, f32[128]{0:T(128)}, u32[]{:S(2)}) copy-start(f32[128]{0:T(128)} %param.21) | copy-start | bytes 1540
  0.0 0.7 %copy-start.12 = (f32[128]{0:T(128)S(1)}, f32[128]{0:T(128)}, u32[]{:S(2)}) copy-start(f32[128]{0:T(128)} %param.22) | copy-start | bytes 1540
  0.0 0.7 %copy-start.6 = (s32[1,4,4]{2,1,0:T(4,128)S(1)}, s32[1,4,4]{2,1,0:T(4,128)}, u32[]{:S(2)}) copy-start(s32[1,4,4]{2,1,0:T(4,128)} %counts_hbm.1) | copy-start | bytes 196
  0.0 0.7 %copy-start.7 = (s32[1,4]{1,0:T(1,128)S(1)}, s32[1,4]{1,0:T(1,128)}, u32[]{:S(2)}) copy-start(s32[1,4]{1,0:T(1,128)} %lengths_hbm.1) | copy-start | bytes 52
  0.0 0.7 %copy-start.8 = (f32[128]{0:T(128)S(1)}, f32[128]{0:T(128)}, u32[]{:S(2)}) copy-start(f32[128]{0:T(128)} %param.17) | copy-start | bytes 1540
  0.0 0.7 %copy-start.9 = (f32[128]{0:T(128)S(1)}, f32[128]{0:T(128)}, u32[]{:S(2)}) copy-start(f32[128]{0:T(128)} %param.18) | copy-start | bytes 1540
  0.8 1.2 %copy-start = (bf16[3,3,3,128,128]{4,3,2,1,0:T(8,128)(2,1)S(1)}, bf16[3,3,3,128,128]{4,3,2,1,0:T(8,128)(2,1)}, u32[]{:S(2)}) copy-start(bf16[3,3,3,128,128]{4,3,2,1,0:T(8,128)(2,1)} %param.20) | copy-start | bytes 2654212
  1.9 1.2 %copy-start.1 = (bf16[3,3,3,128,128]{4,3,2,1,0:T(8,128)(2,1)S(1)}, bf16[3,3,3,128,128]{4,3,2,1,0:T(8,128)(2,1)}, u32[]{:S(2)}) copy-start(bf16[3,3,3,128,128]{4,3,2,1,0:T(8,128)(2,1)} %param.23) | copy-start | bytes 2654212
  3.1 1.0 %copy-start.2 = (s32[768,128]{1,0:T(8,128)S(1)}, s32[768,128]{1,0:T(8,128)}, u32[]{:S(2)}) copy-start(s32[768,128]{1,0:T(8,128)} %constant.2.clone.columns_hbm) | copy-start | bytes 1179652
  4.1 1.0 %copy-start.3 = (bf16[3,3,128,128]{3,2,1,0:T(8,128)(2,1)S(1)}, bf16[3,3,128,128]{3,2,1,0:T(8,128)(2,1)}, u32[]{:S(2)}) copy-start(bf16[3,3,128,128]{3,2,1,0:T(8,128)(2,1)} %param.24) | copy-start | bytes 884740
  5.0 0.7 %copy-start.4 = (bf16[3,3,3,3,128]{4,3,2,1,0:T(4,128)(2,1)S(1)}, bf16[3,3,3,3,128]{4,3,2,1,0:T(4,128)(2,1)}, u32[]{:S(2)}) copy-start(bf16[3,3,3,3,128]{4,3,2,1,0:T(4,128)(2,1)} %in_w_hbm.1) | copy-start | bytes 62212
  5.8 0.7 %copy-start.5 = (bf16[1,1,32,192]{3,2,1,0:T(8,128)(2,1)S(1)}, bf16[1,1,32,192]{3,2,1,0:T(8,128)(2,1)}, u32[]{:S(2)}) copy-start(bf16[1,1,32,192]{3,2,1,0:T(8,128)(2,1)} %pixels_hbm.1) | copy-start | bytes 36868

commit v2 on v1

--- a/solution.py
+++ b/solution.py
@@ -295,14 +295,20 @@
     for j in range(span + 2):
         for kt in range(LAGS):
             lhs[j * HS : (j + 1) * HS, kt * WIDE : (kt + 1) * WIDE] = xrows[picked(j, 2 - kt, 4)]
-    patch = lhs[...]
-    for pair in range(PAIRS):
-        both = jnp.dot(
-            patch, toeplitz[:, pair * 2 * CH : (pair + 1) * 2 * CH], preferred_element_type=F32
-        )
-        for side_at in range(2):
-            part = both[:, side_at * CH : (side_at + 1) * CH] + vecs[0]
-            base[side_at, pl.ds(pair, (span + 2) * HS, stride=PAIRS), :] = part.astype(BF).astype(F32)
+
+    def base_frames(first, amount):
+        patch = lhs[first * HS : (first + amount) * HS, :]
+        for pair in range(PAIRS):
+            both = jnp.dot(
+                patch, toeplitz[:, pair * 2 * CH : (pair + 1) * 2 * CH], preferred_element_type=F32
+            )
+            for side_at in range(2):
+                part = both[:, side_at * CH : (side_at + 1) * CH] + vecs[0]
+                base[side_at, pl.ds(first * HALF + pair, amount * HS, stride=PAIRS), :] = part.astype(
+                    BF
+                ).astype(F32)
+
+    base_frames(2, span)
 
     def frame_stats(even, odd):
         total = jnp.sum(even, axis=0, keepdims=True) + jnp.sum(odd, axis=0, keepdims=True)
@@ -399,6 +405,7 @@
         for j in range(span)
     ]
     stat_copies = share_stats(stats1, 0, rows)
+    base_frames(0, 2)
     means, scales = norm_terms(stats1, 0, stat_copies)
     for j in range(span + 2):
         activate(
@@ -601,7 +608,7 @@
             pltpu.SemaphoreType.DMA((n_dp,)),
         ],
         compiler_params=pltpu.CompilerParams(
-            collective_id=0, has_side_effects=True, vmem_limit_bytes=48 * 1024 * 1024
+            collective_id=0, has_side_effects=True, vmem_limit_bytes=63 * 1024 * 1024
         ),
         name="encoder_block",
     )(

time: 38.2 us -> 32.8 us (0.86)
  local copies, waits for them, and re-layouts: 7.13 us -> 1.57 us
  Pallas kernels: 30.6 us -> 31 us
    unnamed x27 -> x1, local copies, waits for them, and re-layouts: 7.13 us -> 1.57 us
    pallas_call x1, Pallas kernels: 30.6 us -> 31 us  [per_device(): pl.pallas_call(functools.partial(kernel, n_dp, n_tm), out_shape=jax.Shape...]
where the time goes in v2:
time: 32.8 us; the launch traced here: 32.5 us
  Pallas kernels  31 us (95%)
  local copies, waits for them, and re-layouts  1.57 us (5%)
    pallas_call x1, Pallas kernels, per_device(): pl.pallas_call(functools.partial(kernel, n_dp, n_tm), out_shape=jax.Shape...  31 us
    unnamed x1, local copies, waits for them, and re-layouts  1.57 us

profile of v2, /device:TPU:0, one launch (start us, length us, event | category | flops | bytes accessed | tf_op | source)
XLA Modules:
  0.0 32.5 jit_solution(11946354811721357334)
XLA Ops:
  0.0 31.0 %encoder_block.1 = bf16[32,2048]{1,0:T(8,128)(2,1)} custom-call(s32[1,4,4]{2,1,0:T(4,128)} %counts_hbm.1, s32[1,4]{1,0:T(1,128)} %lengths_hbm.1, bf16[1,1,32,192]{3,2,1,0:T(8,128)(2,1)} %pixels_hbm.1, s32[768,128]{1,0:T(8,128)} %constant.2.clone.columns_hbm, bf16[3,3,3,3,128]{4,3,2,1,0:T(4,128)(2,1)} %in_w_hbm.1, f32[1,128]{1,0:T(1,128)} %bitcast.13, ...), custom_call_target="tpu_custom_call" | custom-call | tf_op jit(solution)/shard_map/encoder_block/pallas_call | solution.py:564
  31.0 1.6 %copy.15 = bf16[1,1,32,2048]{3,2,1,0:T(8,128)(2,1)} copy(bf16[1,1,32,2048]{3,2,1,0:T(8,128)(2,1)} %bitcast.11) | data formatting | bytes 262144

commit v3 on v2

--- a/solution.py
+++ b/solution.py
@@ -366,13 +366,14 @@
     blank = jnp.zeros((PAIRS, CH), F32)
 
     def activate(j, source, first, mean, scale, gain, bias):
-        factor = scale * gain
+        factor = scale * (0.5 * gain)
+        shift = 0.5 * bias
         carry = [blank] * 4
         for at in range(0, HALF, PART):
             done = []
             for side_at in range(2):
                 x = source(side_at, first + at)
-                y = 0.5 * ((x - mean) * factor + bias)
+                y = (x - mean) * factor + shift
                 done.append(y + y * jnp.tanh(y))
             even, odd = done
             before = jnp.where(pair_at == 0, 0.0, pltpu.roll(odd, 1, axis=0))
@@ -388,17 +389,24 @@
                 [carry[i], blank], axis=0
             ).astype(BF)
 
-    def conv_frame(j, weight):
+    def conv_frames(frames, weight):
         taps = []
         for kt in range(LAGS):
-            p = picked(j, 2 - kt, 2)
-            taps += [act_a[p, 0:HALF], act_b[p], act_a[p, 2 * PAIRS : 2 * PAIRS + HALF]]
+            picks = [picked(j, 2 - kt, 2) for j in frames]
+            taps += [
+                jnp.concatenate([act_a[p, 0:HALF] for p in picks], axis=0),
+                jnp.concatenate([act_b[p] for p in picks], axis=0),
+                jnp.concatenate([act_a[p, 2 * PAIRS : 2 * PAIRS + HALF] for p in picks], axis=0),
+            ]
         both = jnp.dot(
             jnp.concatenate(taps, axis=1),
             weight[...].reshape(9 * 4 * CH, 2 * CH),
             preferred_element_type=F32,
         )
-        return both[:, :CH], both[:, CH:]
+        return [
+            [both[i * HALF : (i + 1) * HALF, :CH], both[i * HALF : (i + 1) * HALF, CH:]]
+            for i in range(len(frames))
+        ]
 
     rows = [
         frame_stats(*[base[i, (j + 2) * HALF : (j + 3) * HALF, :] for i in range(2)])
@@ -424,17 +432,19 @@
     )
     rows = [None] * span
     order = list(range(span - 2, span)) + list(range(span - 2))
-    for at, j in enumerate(order):
-        pieces = []
-        for i, x in enumerate(conv_frame(j + 2, w1)):
-            x = x.astype(BF)
-            if at < 2:
-                mid_send[at, i] = x
-            x = x.astype(F32)
-            mid[i, j * HALF : (j + 1) * HALF, :] = x
-            pieces.append(x)
-        rows[j] = frame_stats(*pieces)
-        if at == 1:
+    for at in range(0, span, 2):
+        pair = order[at : at + 2]
+        for which, (j, sides) in enumerate(zip(pair, conv_frames([j + 2 for j in pair], w1))):
+            pieces = []
+            for i, x in enumerate(sides):
+                x = x.astype(BF)
+                if at == 0:
+                    mid_send[which, i] = x
+                x = x.astype(F32)
+                mid[i, j * HALF : (j + 1) * HALF, :] = x
+                pieces.append(x)
+            rows[j] = frame_stats(*pieces)
+        if at == 0:
 
             @pl.when(t < n_tm - 1)
             def _():
@@ -469,10 +479,12 @@
         )
     weight_copies[2].wait()
     weight_copies[3].wait()
-    for j in range(span):
-        for i, x in enumerate(conv_frame(j + 2, w2)):
-            x = x + base[i, (j + 2) * HALF : (j + 3) * HALF, :]
-            resid[i, j * HALF : (j + 1) * HALF, :] = x.astype(BF).astype(F32)
+    for at in range(0, span, 2):
+        pair = [at, at + 1]
+        for j, sides in zip(pair, conv_frames([j + 2 for j in pair], w2)):
+            for i, x in enumerate(sides):
+                x = x + base[i, (j + 2) * HALF : (j + 3) * HALF, :]
+                resid[i, j * HALF : (j + 1) * HALF, :] = x.astype(BF).astype(F32)
 
     weight_copies[4].wait()
     cells = span * HALF

time: 32.8 us -> 35 us (1.067)
  Pallas kernels: 31 us -> 33.2 us
    pallas_call x1, Pallas kernels: 31 us -> 33.2 us  [per_device(): pl.pallas_call(functools.partial(kernel, n_dp, n_tm), out_shape=jax.Shape...]
where the time goes in v3:
time: 35 us; the launch traced here: 34.8 us
  Pallas kernels  33.2 us (95%)
  local copies, waits for them, and re-layouts  1.57 us (4%)
    pallas_call x1, Pallas kernels, per_device(): pl.pallas_call(functools.partial(kernel, n_dp, n_tm), out_shape=jax.Shape...  33.2 us
    unnamed x1, local copies, waits for them, and re-layouts  1.57 us

profile of v3, /device:TPU:0, one launch (start us, length us, event | category | flops | bytes accessed | tf_op | source)
XLA Modules:
  0.0 34.8 jit_solution(11857367293993952371)
XLA Ops:
  0.0 33.2 %encoder_block.1 = bf16[32,2048]{1,0:T(8,128)(2,1)} custom-call(s32[1,4,4]{2,1,0:T(4,128)} %counts_hbm.1, s32[1,4]{1,0:T(1,128)} %lengths_hbm.1, bf16[1,1,32,192]{3,2,1,0:T(8,128)(2,1)} %pixels_hbm.1, s32[768,128]{1,0:T(8,128)} %constant.2.clone.columns_hbm, bf16[3,3,3,3,128]{4,3,2,1,0:T(4,128)(2,1)} %in_w_hbm.1, f32[1,128]{1,0:T(1,128)} %bitcast.13, ...), custom_call_target="tpu_custom_call" | custom-call | tf_op jit(solution)/shard_map/encoder_block/pallas_call | solution.py:576
  33.2 1.6 %copy.15 = bf16[1,1,32,2048]{3,2,1,0:T(8,128)(2,1)} copy(bf16[1,1,32,2048]{3,2,1,0:T(8,128)(2,1)} %bitcast.11) | data formatting | bytes 262144
